TPU v7x, 1024 devices: a whole 4x8x16 slice. The times are simulated.
1024 devices in a mesh: gz: 32 (over z_hi, y), gx: 32 (over x, z_lo, core).
Axes of the slice: x: 4, y: 8, z: 16 (z_hi: 4, z_lo: 4; z = z_hi * 4 + z_lo), core: 2. Of those that a mesh axis runs over, the one named last changes fastest.
Arguments:
- phase_field: float32 [256, 1024, 1024], P('gz', 'gx'), may hold values from -1 to 1
- solute: float32 [256, 1024, 1024], P('gz', 'gx'), may hold values from -1 to 0.5
- pull_counts: int32 [2], replicated, may hold values from 1 to 5, as said below
- planes: int32 [32], P('gz'), may hold values from 0 to 255, as said below
Outputs:
- final_phase: float32 [256, 1024, 1024], P('gz', 'gx')
- correlation: float32 [32, 1024, 1024], P('gz', 'gx')
Inputs may be any that keep to these rules, and one draw needn't show every extreme that they name: `pull_counts`: 5 occurs. `planes`: entry s lies between 8 s and 8 s + 7.
All inputs are finite; a program needn't handle non-finite values.
Results may differ from a plain program's by a relative error of at most 0.00021.
Values sent between devices are 32-bit elements; how exact they have to be, the bound alone decides.
A program may use at most 32 MiB of HBM per device.

v0:
```python
import math

import jax
import jax.numpy as jnp
from jax import lax
from jax.sharding import PartitionSpec as P

STEPS = 2
PMAX = 5


TIME_STEP = 0.05
PARTITION = 0.15
COUPLING = 1.6
DIFFUSIVITY = 0.4
FAR_FIELD = -1.0


def shifted(shard, axis, by):
    length = lax.axis_size(axis)
    pairs = [(i, i + by) for i in range(length) if 0 <= i + by < length]
    return lax.ppermute(shard, axis, pairs)


def with_halo(cells, sides, width, closed):
    for axis, dim in sides:
        count = lax.axis_size(axis)
        ends = count if closed else count - 1
        head = lax.slice_in_dim(cells, 0, width, axis=dim)
        tail = lax.slice_in_dim(cells, cells.shape[dim] - width, cells.shape[dim], axis=dim)
        cells = jnp.concatenate(
            [
                lax.ppermute(tail, axis, [(i, (i + 1) % count) for i in range(ends)]),
                cells,
                lax.ppermute(head, axis, [((i + 1) % count, i) for i in range(ends)]),
            ],
            axis=dim,
        )
    return cells


def split_length(length):
    factor = math.isqrt(length)
    while length % factor:
        factor -= 1
    return (length // factor, factor)


def wave_table(count_rows, count_columns, length, direction):
    product = lax.broadcasted_iota(
        jnp.int32, (count_rows, count_columns), 0
    ) * lax.broadcasted_iota(jnp.int32, (count_rows, count_columns), 1)
    phase_angle = direction * 2.0 * math.pi / length * (product % length).astype(jnp.float32)
    return (jnp.cos(phase_angle), jnp.sin(phase_angle))


def contract(pattern, real_part, imag_part, rotation):
    cosine, sine_part = rotation
    highest = lax.Precision.HIGHEST
    real_out = jnp.einsum(pattern, real_part, cosine, precision=highest) - jnp.einsum(
        pattern, imag_part, sine_part, precision=highest
    )
    imag_out = jnp.einsum(pattern, real_part, sine_part, precision=highest) + jnp.einsum(
        pattern, imag_part, cosine, precision=highest
    )
    return (real_out, imag_out)


def rotate(real_part, imag_part, rotation):
    cosine, sine_part = rotation
    return (real_part * cosine - imag_part * sine_part, real_part * sine_part + imag_part * cosine)


def transform_rows(real_part, imag_part, direction):
    length = real_part.shape[-1]
    wide_part, narrow = split_length(length)
    leading = real_part.shape[:-1]
    real_part = real_part.reshape(leading + (narrow, wide_part))
    imag_part = imag_part.reshape(leading + (narrow, wide_part))
    if direction < 0:
        real_part, imag_part = contract(
            "...ba,bk->...ka", real_part, imag_part, wave_table(narrow, narrow, narrow, direction)
        )
        real_part, imag_part = rotate(
            real_part, imag_part, wave_table(narrow, wide_part, length, direction)
        )
        real_part, imag_part = contract(
            "...ka,aj->...kj",
            real_part,
            imag_part,
            wave_table(wide_part, wide_part, wide_part, direction),
        )
    else:
        real_part, imag_part = contract(
            "...kj,aj->...ka",
            real_part,
            imag_part,
            wave_table(wide_part, wide_part, wide_part, direction),
        )
        real_part, imag_part = rotate(
            real_part, imag_part, wave_table(narrow, wide_part, length, direction)
        )
        real_part, imag_part = contract(
            "...ka,bk->...ba", real_part, imag_part, wave_table(narrow, narrow, narrow, direction)
        )
    return (real_part.reshape(leading + (length,)), imag_part.reshape(leading + (length,)))


def close_ends(padded):
    position = lax.axis_index("gz")
    lower_plane = jnp.where(position == 0, padded[:, 1:2], padded[:, :1])
    upper_plane = jnp.where(position == lax.axis_size("gz") - 1, padded[:, -2:-1], padded[:, -1:])
    padded = lax.dynamic_update_slice_in_dim(padded, lower_plane, 0, 1)
    return lax.dynamic_update_slice_in_dim(padded, upper_plane, padded.shape[1] - 1, 1)


def pull_frame(phase_now, solute_now, phase_depth, solute_depth):
    payload = jnp.concatenate([phase_now[:phase_depth], solute_now[:solute_depth]], 0)
    arrived = shifted(payload, "gz", -1)
    at_top = lax.axis_index("gz") == lax.axis_size("gz") - 1
    arrived = jnp.where(at_top, FAR_FIELD, arrived)
    phase_ext = jnp.concatenate([phase_now, arrived[:phase_depth]], 0)
    solute_ext = jnp.concatenate([solute_now, arrived[phase_depth:]], 0)
    return (phase_ext, solute_ext)


def advance(padded, solute_now, thermal, with_solute):
    fields = padded[:, 1:-1]
    centre = fields[0]
    widened = with_halo(fields, (("gx", 2),), 1, True)
    beside = [
        padded[:, :-2],
        padded[:, 2:],
        widened[:, :, :-2],
        widened[:, :, 2:],
        jnp.roll(fields, 1, 3),
        jnp.roll(fields, -1, 3),
    ]
    laplace = sum((neighbour[0] for neighbour in beside)) - 6.0 * centre
    driving = (
        laplace
        + centre
        - centre * centre * centre
        - COUPLING * (1.0 - centre * centre) * (1.0 - centre * centre) * (solute_now + thermal)
    )
    phase_next = jnp.clip(centre + TIME_STEP * driving, -1.0, 1.0)
    if not with_solute:
        return (phase_next, solute_now)
    mobility = 0.5 * (1.0 - centre)
    solute_flux = sum(
        (
            0.5 * (mobility + 0.5 * (1.0 - neighbour[0])) * (neighbour[1] - solute_now)
            for neighbour in beside
        )
    )
    solute_rate = (
        DIFFUSIVITY * solute_flux + 0.5 * (1.0 + (1.0 - PARTITION) * solute_now) * driving
    ) / (0.5 * (1.0 + PARTITION) - 0.5 * (1.0 - PARTITION) * centre)
    return (phase_next, solute_now + TIME_STEP * solute_rate)


def per_device(phase_field, solute, pull_counts, planes):
    depth_here = phase_field.shape[0]
    position = lax.axis_index("gz")
    total_height = depth_here * lax.axis_size("gz")
    heights = (position * depth_here + lax.iota(jnp.int32, depth_here)).astype(jnp.float32)
    thermal = ((2.0 * heights - total_height) / total_height)[:, None, None]
    phase_now, solute_now = (phase_field, solute)
    for step_index in range(STEPS):
        with_solute = step_index < STEPS - 1
        pull_now = pull_counts[step_index]
        phase_ext, solute_ext = pull_frame(phase_now, solute_now, PMAX, PMAX)
        phase_now = lax.dynamic_slice_in_dim(phase_ext, pull_now, depth_here, 0)
        solute_now = lax.dynamic_slice_in_dim(solute_ext, pull_now, depth_here, 0)
        fields = jnp.stack([phase_now, solute_now]) if with_solute else phase_now[None]
        padded = close_ends(with_halo(fields, (("gz", 1),), 1, False))
        phase_now, solute_now = advance(padded, solute_now, thermal, with_solute)
    local_index = planes - position * depth_here
    sample = jnp.take(phase_now, local_index, axis=0)
    row_real, row_imag = transform_rows(sample, jnp.zeros_like(sample), -1.0)
    cells_plane = phase_field.shape[1] * lax.axis_size("gx") * phase_field.shape[2]
    norm_factor = 1.0 / (cells_plane * math.sqrt(cells_plane))
    halves = (
        lax.all_to_all(row_real, "gx", split_axis=2, concat_axis=1, tiled=True),
        lax.all_to_all(row_imag, "gx", split_axis=2, concat_axis=1, tiled=True),
    )
    real_part = jnp.swapaxes(halves[0], 1, 2)
    imag_part = jnp.swapaxes(halves[1], 1, 2)
    real_part, imag_part = transform_rows(real_part, imag_part, -1.0)
    spectral_power = real_part * real_part + imag_part * imag_part
    column_index = lax.axis_index("gx") * spectral_power.shape[1] + lax.broadcasted_iota(
        jnp.int32, spectral_power.shape, 1
    )
    row_index = lax.broadcasted_iota(jnp.int32, spectral_power.shape, 2)
    spectral_power = jnp.where((column_index == 0) & (row_index == 0), 0.0, spectral_power)
    real_part, imag_part = transform_rows(spectral_power, jnp.zeros_like(spectral_power), 1.0)
    halves = (
        lax.all_to_all(
            jnp.swapaxes(real_part, 1, 2), "gx", split_axis=1, concat_axis=2, tiled=True
        ),
        lax.all_to_all(
            jnp.swapaxes(imag_part, 1, 2), "gx", split_axis=1, concat_axis=2, tiled=True
        ),
    )
    finish_real_part, finish_imag_part = transform_rows(halves[0], halves[1], 1.0)
    correlation = finish_real_part * norm_factor
    return (phase_now, correlation)


def solution(mesh):
    return jax.shard_map(
        per_device,
        mesh=mesh,
        in_specs=(P("gz", "gx", None), P("gz", "gx", None), P(), P("gz")),
        out_specs=(P("gz", "gx", None), P("gz", "gx", None)),
        check_vma=False,
    )
```

profile of v0, /device:TPU:569, one launch (start us, length us, event | category | flops | bytes accessed | tf_op | source)
XLA Modules:
  0.0 413.6 jit_solution(326414277169662613)
XLA Ops:
  2.1 3.0 collective-permute-start
  7.6 149.0 %collective-permute-done = f32[10,32,1024]{2,1,0:T(8,128)S(1)} collective-permute-done((f32[10,32,1024]{2,1,0:T(8,128)S(1)}, f32[10,32,1024]{2,1,0:T(8,128)S(1)}, u32[]{:S(2)}, u32[]{:S(2)}) %collective-permute-start) | collective-permute-done | bytes 1310752 | tf_op jit(solution)/shard_map/ppermute | solution.py:22
  158.6 1.9 collective-permute-start.1
  160.5 3.4 collective-permute-start.2
  163.9 2.8 collective-permute-done.1
  166.7 32.3 %collective-permute-done.2 = f32[2,1,32,1024]{3,2,1,0:T(8,128)S(1)} collective-permute-done((f32[2,1,32,1024]{3,2,1,0:T(8,128)S(1)}, f32[2,1,32,1024]{3,2,1,0:T(8,128)S(1)}, u32[]{:S(2)}, u32[]{:S(2)}) %collective-permute-start.2) | collective-permute-done | bytes 262176 | tf_op jit(solution)/shard_map/ppermute | solution.py:35
  200.3 1.9 collective-permute-start.3
  202.3 2.7 collective-permute-start.4
  205.3 2.5 collective-permute-done.4
  208.9 3.3 multiply_add_fusion
  212.3 1.2 pad_maximum_fusion.2
  213.5 1.9 collective-permute-start.5
  217.4 81.1 %collective-permute-done.5 = f32[10,32,1024]{2,1,0:T(8,128)} collective-permute-done((f32[10,32,1024]{2,1,0:T(8,128)}, f32[10,32,1024]{2,1,0:T(8,128)}, u32[]{:S(2)}, u32[]{:S(2)}) %collective-permute-start.5) | collective-permute-done | bytes 1310752 | tf_op jit(solution)/shard_map/ppermute | solution.py:22
  298.5 1.4 broadcast_select_fusion
  301.1 1.9 collective-permute-start.6
  303.1 3.4 collective-permute-start.7
  307.2 7.6 %collective-permute-done.7 = f32[1,1,32,1024]{3,2,1,0:T(8,128)S(1)} collective-permute-done((f32[1,1,32,1024]{3,2,1,0:T(8,128)S(1)}, f32[1,1,32,1024]{3,2,1,0:T(8,128)S(1)}, u32[]{:S(2)}, u32[]{:S(2)}) %collective-permute-start.7) | collective-permute-done | bytes 131104 | tf_op jit(solution)/shard_map/ppermute | solution.py:35
  315.4 2.1 collective-permute-start.8
  317.5 4.5 %collective-permute-start.9 = (f32[1,8,1,1024]{3,2,1,0:T(1,128)S(1)}, f32[1,8,1,1024]{3,2,1,0:T(1,128)S(1)}, u32[]{:S(2)}, u32[]{:S(2)}) collective-permute-start(f32[1,8,1,1024]{3,2,1,0:T(1,128)S(1)} %get-tuple-element.26), channel_id=1, source_target_pairs={{1,0},{2,1},{3,2},{4,3},{5,4},{6,5},{7,6},{8,7},{9,8},{10,9},{11,1... | collective-permute-start | bytes 98312 | tf_op jit(solution)/shard_map/ppermute | solution.py:35
  322.7 1.2 fusion.18
  329.6 1.9 reduce
  332.5 13.8 %all-to-all-start = ((f32[32,1,1024]{2,1,0:T(1,128)}), f32[32,1,1024]{2,1,0:T(1,128)S(1)}, u32[]{:S(2)}, u32[]{:S(2)}) async-start(f32[32,1,1024]{2,1,0:T(1,128)} %reshape.344), calls=%async_computation | async-start | bytes 262144 | tf_op jit(solution)/shard_map/all_to_all | solution.py:184
  347.9 1.9 reduce.2
  350.8 4.2 %all-to-all-done = f32[32,1,1024]{2,1,0:T(1,128)S(1)} async-done(((f32[32,1,1024]{2,1,0:T(1,128)}), f32[32,1,1024]{2,1,0:T(1,128)S(1)}, u32[]{:S(2)}, u32[]{:S(2)}) %all-to-all-start) | async-done | bytes 131104 | tf_op jit(solution)/shard_map/all_to_all | solution.py:184
  355.0 4.1 all-to-all-start.1
  363.1 4.6 %all-to-all-done.1 = f32[32,1,1024]{2,1,0:T(1,128)S(1)} async-done(((f32[32,1,1024]{2,1,0:T(1,128)}), f32[32,1,1024]{2,1,0:T(1,128)S(1)}, u32[]{:S(2)}, u32[]{:S(2)}) %all-to-all-start.1) | async-done | bytes 131104 | tf_op jit(solution)/shard_map/all_to_all | solution.py:185
  378.8 1.9 reduce.4
  381.7 3.9 all-to-all-start.2
  387.3 1.9 reduce.6
  390.1 4.3 %all-to-all-done.2 = f32[32,1,1024]{2,1,0:T(1,128)S(1)} async-done(((f32[32,1,1024]{2,1,0:T(1,128)}), f32[32,1,1024]{2,1,0:T(1,128)S(1)}, u32[]{:S(2)}, u32[]{:S(2)}) %all-to-all-start.2) | async-done | bytes 131104 | tf_op jit(solution)/shard_map/all_to_all | solution.py:198
  394.4 4.3 %all-to-all-start.3 = ((f32[32,1,1024]{2,1,0:T(1,128)}), f32[32,1,1024]{2,1,0:T(1,128)S(1)}, u32[]{:S(2)}, u32[]{:S(2)}) async-start(f32[32,1,1024]{2,1,0:T(1,128)} %reshape.350), calls=%async_computation.3 | async-start | bytes 262144 | tf_op jit(solution)/shard_map/all_to_all | solution.py:201
  402.4 5.0 %all-to-all-done.3 = f32[32,1,1024]{2,1,0:T(1,128)S(1)} async-done(((f32[32,1,1024]{2,1,0:T(1,128)}), f32[32,1,1024]{2,1,0:T(1,128)S(1)}, u32[]{:S(2)}, u32[]{:S(2)}) %all-to-all-start.3) | async-done | bytes 131104 | tf_op jit(solution)/shard_map/all_to_all | solution.py:201
  (106 shorter events, 46.5 us)
Async XLA Ops:
  0.6 1.1 slice-start
  0.6 1.3 slice-start.1
  0.7 4.4 %copy-start.4 = (s32[2]{0:T(128)S(1)}, s32[2]{0:T(128)}, u32[]{:S(2)}) copy-start(s32[2]{0:T(128)} %param.6) | copy-start | bytes 28
  2.1 154.5 %collective-permute-start = (f32[10,32,1024]{2,1,0:T(8,128)S(1)}, f32[10,32,1024]{2,1,0:T(8,128)S(1)}, u32[]{:S(2)}, u32[]{:S(2)}) collective-permute-start(f32[10,32,1024]{2,1,0:T(8,128)S(1)} %pad_maximum_fusion.1), channel_id=1, source_target_pairs={{32,0},{64,32},{96,64},{128,96},{160,128},{192,160},{224,192},{256... | collective-permute-start | bytes 3932168 | tf_op jit(solution)/shard_map/ppermute | solution.py:22
  156.8 1.2 copy-start
  156.9 1.4 copy-start.1
  158.6 8.1 %collective-permute-start.1 = (f32[2,1,32,1024]{3,2,1,0:T(8,128)S(1)}, f32[2,1,32,1024]{3,2,1,0:T(8,128)S(1)}, u32[]{:S(2)}, u32[]{:S(2)}) collective-permute-start(f32[2,1,32,1024]{3,2,1,0:T(8,128)S(1)} %get-tuple-element.19), channel_id=1, source_target_pairs={{0,32},{32,64},{64,96},{96,128},{128,160},{160,192},{192,224},{224... | collective-permute-start | bytes 786440 | tf_op jit(solution)/shard_map/ppermute | solution.py:33
  160.5 38.5 %collective-permute-start.2 = (f32[2,1,32,1024]{3,2,1,0:T(8,128)S(1)}, f32[2,1,32,1024]{3,2,1,0:T(8,128)S(1)}, u32[]{:S(2)}, u32[]{:S(2)}) collective-permute-start(f32[2,1,32,1024]{3,2,1,0:T(8,128)S(1)} %get-tuple-element.20), channel_id=1, source_target_pairs={{32,0},{64,32},{96,64},{128,96},{160,128},{192,160},{224,192},{256... | collective-permute-start | bytes 786440 | tf_op jit(solution)/shard_map/ppermute | solution.py:35
  200.3 5.0 %collective-permute-start.3 = (f32[2,8,1,1024]{3,2,1,0:T(1,128)S(1)}, f32[2,8,1,1024]{3,2,1,0:T(1,128)S(1)}, u32[]{:S(2)}, u32[]{:S(2)}) collective-permute-start(f32[2,8,1,1024]{3,2,1,0:T(1,128)S(1)} %get-tuple-element.13), channel_id=1, source_target_pairs={{0,1},{1,2},{2,3},{3,4},{4,5},{5,6},{6,7},{7,8},{8,9},{9,10},{10,1... | collective-permute-start | bytes 196616 | tf_op jit(solution)/shard_map/ppermute | solution.py:33
  202.3 5.6 %collective-permute-start.4 = (f32[2,8,1,1024]{3,2,1,0:T(1,128)S(1)}, f32[2,8,1,1024]{3,2,1,0:T(1,128)S(1)}, u32[]{:S(2)}, u32[]{:S(2)}) collective-permute-start(f32[2,8,1,1024]{3,2,1,0:T(1,128)S(1)} %get-tuple-element.14), channel_id=1, source_target_pairs={{1,0},{2,1},{3,2},{4,3},{5,4},{6,5},{7,6},{8,7},{9,8},{10,9},{11,1... | collective-permute-start | bytes 196616 | tf_op jit(solution)/shard_map/ppermute | solution.py:35
  213.5 85.0 %collective-permute-start.5 = (f32[10,32,1024]{2,1,0:T(8,128)}, f32[10,32,1024]{2,1,0:T(8,128)}, u32[]{:S(2)}, u32[]{:S(2)}) collective-permute-start(f32[10,32,1024]{2,1,0:T(8,128)} %pad_maximum_fusion.2), channel_id=1, source_target_pairs={{32,0},{64,32},{96,64},{128,96},{160,128},{192,160},{224,192},{256... | collective-permute-start | bytes 3932168 | tf_op jit(solution)/shard_map/ppermute | solution.py:22
  301.1 6.1 %collective-permute-start.6 = (f32[1,1,32,1024]{3,2,1,0:T(8,128)S(1)}, f32[1,1,32,1024]{3,2,1,0:T(8,128)S(1)}, u32[]{:S(2)}, u32[]{:S(2)}) collective-permute-start(f32[1,1,32,1024]{3,2,1,0:T(8,128)S(1)} %get-tuple-element.31), channel_id=1, source_target_pairs={{0,32},{32,64},{64,96},{96,128},{128,160},{160,192},{192,224},{224... | collective-permute-start | bytes 393224 | tf_op jit(solution)/shard_map/ppermute | solution.py:33
  303.1 11.7 %collective-permute-start.7 = (f32[1,1,32,1024]{3,2,1,0:T(8,128)S(1)}, f32[1,1,32,1024]{3,2,1,0:T(8,128)S(1)}, u32[]{:S(2)}, u32[]{:S(2)}) collective-permute-start(f32[1,1,32,1024]{3,2,1,0:T(8,128)S(1)} %get-tuple-element.32), channel_id=1, source_target_pairs={{32,0},{64,32},{96,64},{128,96},{160,128},{192,160},{224,192},{256... | collective-permute-start | bytes 393224 | tf_op jit(solution)/shard_map/ppermute | solution.py:35
  315.4 7.3 %copy-start.2 = (f32[5,32,1024]{2,1,0:T(8,128)S(1)}, f32[5,32,1024]{2,1,0:T(8,128)}, u32[]{:S(2)}) copy-start(f32[5,32,1024]{2,1,0:T(8,128)} %get-tuple-element.28) | copy-start | bytes 1966084
  315.4 6.8 %collective-permute-start.8 = (f32[1,8,1,1024]{3,2,1,0:T(1,128)S(1)}, f32[1,8,1,1024]{3,2,1,0:T(1,128)S(1)}, u32[]{:S(2)}, u32[]{:S(2)}) collective-permute-start(f32[1,8,1,1024]{3,2,1,0:T(1,128)S(1)} %get-tuple-element.25), channel_id=1, source_target_pairs={{0,1},{1,2},{2,3},{3,4},{4,5},{5,6},{6,7},{7,8},{8,9},{9,10},{10,1... | collective-permute-start | bytes 98312 | tf_op jit(solution)/shard_map/ppermute | solution.py:33
  317.5 5.2 %collective-permute-start.9 = (f32[1,8,1,1024]{3,2,1,0:T(1,128)S(1)}, f32[1,8,1,1024]{3,2,1,0:T(1,128)S(1)}, u32[]{:S(2)}, u32[]{:S(2)}) collective-permute-start(f32[1,8,1,1024]{3,2,1,0:T(1,128)S(1)} %get-tuple-element.26), channel_id=1, source_target_pairs={{1,0},{2,1},{3,2},{4,3},{5,4},{6,5},{7,6},{8,7},{9,8},{10,9},{11,1... | collective-permute-start | bytes 98312 | tf_op jit(solution)/shard_map/ppermute | solution.py:35
  323.9 1.0 copy-start.3
  332.5 22.5 %all-to-all-start = ((f32[32,1,1024]{2,1,0:T(1,128)}), f32[32,1,1024]{2,1,0:T(1,128)S(1)}, u32[]{:S(2)}, u32[]{:S(2)}) async-start(f32[32,1,1024]{2,1,0:T(1,128)} %reshape.344), calls=%async_computation | async-start | bytes 262144 | tf_op jit(solution)/shard_map/all_to_all | solution.py:184
  355.0 12.7 %all-to-all-start.1 = ((f32[32,1,1024]{2,1,0:T(1,128)}), f32[32,1,1024]{2,1,0:T(1,128)S(1)}, u32[]{:S(2)}, u32[]{:S(2)}) async-start(f32[32,1,1024]{2,1,0:T(1,128)} %reshape.346), calls=%async_computation.1 | async-start | bytes 262144 | tf_op jit(solution)/shard_map/all_to_all | solution.py:185
  381.7 12.7 %all-to-all-start.2 = ((f32[32,1,1024]{2,1,0:T(1,128)}), f32[32,1,1024]{2,1,0:T(1,128)S(1)}, u32[]{:S(2)}, u32[]{:S(2)}) async-start(f32[32,1,1024]{2,1,0:T(1,128)} %reshape.348), calls=%async_computation.2 | async-start | bytes 262144 | tf_op jit(solution)/shard_map/all_to_all | solution.py:198
  394.4 13.0 %all-to-all-start.3 = ((f32[32,1,1024]{2,1,0:T(1,128)}), f32[32,1,1024]{2,1,0:T(1,128)S(1)}, u32[]{:S(2)}, u32[]{:S(2)}) async-start(f32[32,1,1024]{2,1,0:T(1,128)} %reshape.350), calls=%async_computation.3 | async-start | bytes 262144 | tf_op jit(solution)/shard_map/all_to_all | solution.py:201
where the time goes:
time: 420 us; the launch traced here: 414 us
  waiting for transfers between devices  294 us (70%)
  starting transfers between devices  52.7 us (13%)
  other arithmetic  21.2 us (5%)
  matrix products  20.9 us (5%)
  local copies, waits for them, and re-layouts  18.8 us (4%)
  between operations  6.25 us (1%)
    ppermute x2, waiting for transfers between devices, shifted(): return lax.ppermute(shard, axis, pairs)  230 us
    ppermute x4, waiting for transfers between devices, with_halo(): lax.ppermute(head, axis, [((i + 1) % count, i) for i in range(ends)])  42.9 us
    ppermute x4, starting transfers between devices, with_halo(): lax.ppermute(head, axis, [((i + 1) % count, i) for i in range(ends)])  13.9 us
    all_to_all x1, starting transfers between devices, per_device(): lax.all_to_all(row_real, 'gx', split_axis=2, concat_axis=1, tiled=True)  13.8 us
    unnamed x19, local copies, waits for them, and re-layouts  10 us
  transfers between devices with their start and end apart: 14, of which 11 were waited for; matrix products, arithmetic and copies ran while one was open for 4% of the time, Pallas kernels for 0%

commit v1 on v0

v1 whole, which is shorter than its diff:
```python
import functools
import math

import jax
import jax.numpy as jnp
import ml_dtypes
import numpy as np
from jax import lax
from jax.experimental import pallas as pl
from jax.experimental.pallas import tpu as pltpu
from jax.sharding import PartitionSpec as P

MESH = pl.DeviceIdType.MESH
F32 = jnp.float32
BF16 = jnp.bfloat16

TIME_STEP = 0.05
PARTITION = 0.15
COUPLING = 1.6
DIFFUSIVITY = 0.4
FAR = -1.0

NP, NR, NL = 8, 32, 1024
HALF = NL // 2
RUN = 8
TOP = 8
PIECE = (8, 128)


def split_bf16(table):
    high = table.astype(ml_dtypes.bfloat16)
    low = (table - high.astype(np.float64)).astype(ml_dtypes.bfloat16)
    return np.stack([high, low])


@functools.lru_cache(None)
def tables():
    w = 2.0 * math.pi / NL
    parts, part_rows = 16, 32
    m = np.arange(parts)[:, None]
    l = np.arange(part_rows)[None, :]
    order = np.arange(HALF)
    near = np.arange(HALF)

    def trig(a, b):
        angle = (a[:, None] * b[None, :]) % NL
        return np.cos(w * angle), np.sin(w * angle)

    w1, w2 = [], []
    for odd in (0, 1):
        ky = np.broadcast_to(2 * (16 * m + l % 16) + odd, (parts, part_rows)).reshape(-1)
        imag = np.broadcast_to(l >= 16, (parts, part_rows)).reshape(-1)
        c, s = trig(near, ky)
        fwd = np.where(imag[None, :], -s, c)
        inv = 2.0 * np.where(imag[None, :], -s, c)
        if not odd:
            fwd[:, 16] = (-1.0) ** near
            inv[:, 0] = 1.0
            inv[:, 16] = (-1.0) ** near
        w1.append(fwd)
        inv = inv.reshape(HALF, parts, 4, 8).transpose(0, 2, 1, 3).reshape(HALF, HALF)
        w2.append(inv.T / (NL * NL * float(NL)))
    g, i, r = np.meshgrid(np.arange(4), np.arange(parts), np.arange(8), indexing="ij")
    x = (32 * i + 8 * g + r).reshape(-1)
    cs, back = [], []
    for odd in (0, 1):
        kx = 2 * order + odd
        cs.append(np.concatenate(trig(x, kx), 1))
        back.append(np.concatenate(trig(kx, near), 1))
    return tuple(split_bf16(np.stack(t)) for t in (w1, cs, back, w2))


def mm(x, table, odd):
    rows = x.shape[0]
    high = x.astype(BF16)
    low = (x - high.astype(F32)).astype(BF16)
    both = jnp.concatenate([high, low], 0)
    first = jnp.dot(both, table[0, odd], preferred_element_type=F32)
    second = jnp.dot(high, table[1, odd], preferred_element_type=F32)
    return first[:rows] + first[rows:] + second


def pack(block, out):
    lane_group = lax.broadcasted_iota(jnp.int32, PIECE, 1) // 32
    for c in range(8):
        v = [block[8 * g : 8 * g + 8, 128 * c : 128 * c + 128] for g in range(4)]
        for b in range(4):
            tile = v[b]
            for g in range(4):
                if g != b:
                    moved = pltpu.roll(v[g], (32 * (g - b)) % 128, 1)
                    tile = jnp.where(lane_group == g, moved, tile)
            if b:
                pass
            out[4 * c + b] = tile


def unpack(tiles):
    flat = tiles[...].reshape(256, 128)
    turned = flat.T
    return jnp.concatenate([turned[32 * g : 32 * g + 32] for g in range(4)], 1)


def seam_columns(run):
    return (0, run - 1, run // 2 - 1, run // 2)


class Message:
    def __init__(self, env, index, up, src, dst):
        self.src, self.dst, self.up = src, dst, up
        self.sems = [env["msem"].at[index, j] for j in range(4)]
        self.relay_ref = env["ra"][index]
        self.run, self.height = env["run"], env["height"]
        self.y = (self.run - 1 - env["y"]) if up else env["y"]
        self.h = (self.height - 1 - env["h"]) if up else env["h"]
        self.columns = seam_columns(self.run)

    def copy(self, src, dst, send, recv, y, h):
        if self.up:
            y, h = self.run - 1 - y, self.height - 1 - h
        return pltpu.make_async_remote_copy(
            src_ref=src,
            dst_ref=dst,
            send_sem=self.sems[send],
            recv_sem=self.sems[recv],
            device_id={"gz": h * self.run + y},
            device_id_type=MESH,
        )

    def rows(self, ref, g):
        return ref.at[:, 8 * g : 8 * g + 8, :]

    def has_target(self):
        return jnp.logical_or(self.y > 0, self.h > 0)

    def has_source(self):
        return jnp.logical_or(self.y < self.run - 1, self.h < self.height - 1)

    def start(self):
        self.start_seam()
        self.start_inside()

    def start_inside(self):
        @pl.when(self.y > 0)
        def _():
            self.copy(self.src, self.dst, 0, 1, self.y - 1, self.h).start()

    def start_seam(self):
        @pl.when(jnp.logical_and(self.y == 0, self.h > 0))
        def _():
            for g in (2, 3, 1):
                column = self.columns[g]
                self.copy(self.rows(self.src, g), self.relay_ref, 0, 3, column, self.h).start()
            end = self.run - 1
            self.copy(self.rows(self.src, 0), self.rows(self.dst, 0), 0, 1, end, self.h - 1).start()

    def relay(self, groups=(1, 2, 3)):
        end = self.run - 1
        for g in groups:

            @pl.when(jnp.logical_and(self.h > 0, self.y == self.columns[g]))
            def _(g=g):
                self.copy(self.relay_ref, self.relay_ref, 2, 3, end, self.h - 1).wait_recv()
                there = self.rows(self.dst, g)
                self.copy(self.relay_ref, there, 2, 1, end, self.h - 1).start()

    def arrive(self):
        @pl.when(self.has_source())
        def _():
            self.copy(self.src, self.dst, 0, 1, 0, 0).wait_recv()

    def finish(self):
        @pl.when(self.has_target())
        def _():
            self.copy(self.src, self.dst, 0, 1, 0, 0).wait_send()

        column = [self.y == self.columns[g] for g in (1, 2, 3)]

        @pl.when(jnp.logical_and(self.h > 0, functools.reduce(jnp.logical_or, column)))
        def _():
            self.copy(self.relay_ref, self.relay_ref, 2, 3, 0, 0).wait_send()


MESSAGES = (3, 3, 1, 1, 2, 4, 2, 2)


def lane_sides(v):
    return pltpu.roll(v, 1, 1), pltpu.roll(v, NL - 1, 1)


def driving_of(centre, total, solute_now, thermal):
    gap = 1.0 - centre * centre
    return (total - 6.0 * centre) + centre * gap - COUPLING * (gap * gap) * (solute_now + thermal)


def advance_phase(centre, driving):
    return jnp.clip(centre + TIME_STEP * driving, -1.0, 1.0)


NAMES = (
    "pulls", "plane", "phase", "solute", "w1", "cs", "back", "w2", "final", "corr", "ph", "so",
    "p1", "s1", "fb", "hsd", "hsu", "hrd", "hru", "xsl", "xsh", "xrl", "xrh", "cse", "csu",
    "cre", "cru", "ixs", "ixa", "ixb", "c2s", "c2r", "c1s", "c1r", "sd1", "rv1", "sd2", "rv2",
    "v1", "vcs", "vback", "v2",
    *["ra%d" % n for n in range(8)],
    "msem", "osem", "lsem",
)


def kernel(run, with_corr, *refs):
    r = dict(zip(NAMES, refs, strict=True))
    k = lax.axis_index("gz")
    i = lax.axis_index("gx")
    count_z, count_x = lax.axis_size("gz"), lax.axis_size("gx")
    height = count_z // run
    y, h = lax.rem(k, run), lax.div(k, run)
    at_top = k == count_z - 1
    ph, so, p1, s1, fb = (r[n] for n in ("ph", "so", "p1", "s1", "fb"))
    lsem, osem = r["lsem"], r["osem"]

    own = slice(TOP, TOP + NR)
    load_phase = pltpu.make_async_copy(r["phase"], ph.at[2 : 2 + NP, own, :], lsem.at[0])
    load_solute = pltpu.make_async_copy(r["solute"], so.at[1 : 1 + NP, own, :], lsem.at[1])
    stage = [
        pltpu.make_async_copy(r["phase"].at[0:2], r["hsd"].at[0:2], lsem.at[6]),
        pltpu.make_async_copy(r["solute"].at[0:1], r["hsd"].at[2:3], lsem.at[7]),
        pltpu.make_async_copy(r["phase"].at[NP - 2 : NP], r["hsu"].at[0:2], lsem.at[8]),
        pltpu.make_async_copy(r["solute"].at[NP - 1 : NP], r["hsu"].at[2:3], lsem.at[9]),
    ]
    loads = [
        pltpu.make_async_copy(r[a], r[b], lsem.at[2 + n])
        for n, (a, b) in enumerate((("w1", "v1"), ("cs", "vcs"), ("back", "vback"), ("w2", "v2")))
    ]
    for copy in (load_phase, load_solute, *stage, *loads):
        copy.start()

    barrier = pltpu.get_barrier_semaphore()

    def greet_x(j, carry):
        other = lax.rem(i + j, count_x)
        pl.semaphore_signal(barrier, inc=1, device_id={"gx": other}, device_id_type=MESH)
        return carry

    lax.fori_loop(1, count_x, greet_x, 0)

    def greet_y(j, carry):
        other = h * run + lax.rem(y + j, run)
        pl.semaphore_signal(barrier, inc=1, device_id={"gz": other}, device_id_type=MESH)
        return carry

    lax.fori_loop(1, run, greet_y, 0)
    def is_column(up):
        return functools.reduce(jnp.logical_or, [y == (run - 1 - c if up else c) for c in seam_columns(run)])

    def greet(other):
        pl.semaphore_signal(barrier, inc=1, device_id={"gz": other}, device_id_type=MESH)

    greetings = (count_x - 1) + (run - 1)
    for up in (False, True):
        near, far = (h < height - 1, h > 0) if up else (h > 0, h < height - 1)
        step = 1 if up else -1
        last = 0 if up else run - 1

        @pl.when(jnp.logical_and(near, is_column(up)))
        def _(step=step, last=last):
            greet((h + step) * run + last)

        @pl.when(jnp.logical_and(far, y == last))
        def _(up=up, step=step):
            for c in seam_columns(run):
                greet((h - step) * run + (run - 1 - c if up else c))

        greetings = greetings + jnp.where(jnp.logical_and(near, is_column(up)), 1, 0)
        greetings = greetings + jnp.where(jnp.logical_and(far, y == last), 4, 0)

    load_phase.wait()
    load_solute.wait()
    for copy in stage:
        copy.wait()
    for p in range(NP):
        at = slice(p, p + 1)
        r["xsl"][0, at, :] = ph[p + 2, TOP : TOP + 1, :]
        r["xsl"][1, at, :] = ph[p + 2, TOP + 1 : TOP + 2, :]
        r["xsl"][2, at, :] = so[p + 1, TOP : TOP + 1, :]
        r["xsh"][0, at, :] = ph[p + 2, TOP + NR - 1 : TOP + NR, :]
        r["xsh"][1, at, :] = ph[p + 2, TOP + NR - 2 : TOP + NR - 1, :]
        r["xsh"][2, at, :] = so[p + 1, TOP + NR - 1 : TOP + NR, :]
    r["ixs"][...] = jnp.full(PIECE, r["plane"][0], jnp.int32)

    pl.semaphore_wait(barrier, greetings)

    env = {
        "msem": r["msem"],
        "ra": [r["ra%d" % n] for n in range(8)],
        "run": run,
        "height": height,
        "y": y,
        "h": h,
    }
    down = Message(env, 0, False, r["hsd"], r["hrd"])
    upward = Message(env, 1, True, r["hsu"], r["hru"])
    second = Message(env, 2, False, r["c2s"], r["c2r"])
    first = Message(env, 3, False, r["c1s"], r["c1r"])
    bulk = [
        Message(env, 4, False, fb.at[0:2], fb.at[8:10]),
        Message(env, 5, False, fb.at[2:6], fb.at[10:14]),
        Message(env, 6, False, fb.at[6:8], fb.at[14:16]),
    ]
    onward = Message(env, 7, False, fb.at[8:10], fb.at[16:18])

    def remote(src, dst, n, target):
        return pltpu.make_async_remote_copy(
            src_ref=src,
            dst_ref=dst,
            send_sem=osem.at[2 * n],
            recv_sem=osem.at[2 * n + 1],
            device_id=target,
            device_id_type=MESH,
        )

    above = {"gz": lax.rem(k + 1, count_z)}
    below = {"gz": lax.rem(k + count_z - 1, count_z)}
    not_top = jnp.logical_not(at_top)
    not_low = k > 0

    down.start_seam()
    upward.start_seam()
    before = {"gx": lax.rem(i + count_x - 1, count_x)}
    after = {"gx": lax.rem(i + 1, count_x)}
    to_before = remote(r["xsl"], r["xrh"], 0, before)
    to_after = remote(r["xsh"], r["xrl"], 1, after)
    to_before.start()
    to_after.start()
    index_first = remote(r["ixs"], r["ixa"], 2, above)
    index_second = remote(r["ixa"], r["ixb"], 3, above)

    @pl.when(not_top)
    def _():
        index_first.start()

    to_before.wait_recv()
    to_after.wait_recv()
    r["cse"][0:1, :] = r["xrl"][0, 0:1, :]
    r["cse"][1:2, :] = r["xrh"][0, 0:1, :]
    r["csu"][0:1, :] = r["xrl"][0, NP - 1 : NP, :]
    r["csu"][1:2, :] = r["xrh"][0, NP - 1 : NP, :]
    corner_down = remote(r["cse"], r["cre"], 4, below)
    corner_up = remote(r["csu"], r["cru"], 5, above)

    @pl.when(not_low)
    def _():
        corner_down.start()

    @pl.when(not_top)
    def _():
        corner_up.start()

    down.relay()
    upward.relay()
    down.start_inside()
    upward.start_inside()

    for p in range(NP):
        ph[p + 2, TOP - 1 : TOP, :] = r["xrl"][0, p : p + 1, :]
        ph[p + 2, TOP + NR : TOP + NR + 1, :] = r["xrh"][0, p : p + 1, :]

    @pl.when(not_low)
    def _():
        index_first.wait_recv()

    @pl.when(jnp.logical_and(not_top, not_low))
    def _():
        index_second.start()

    pull_first = r["pulls"][0]
    pull_both = pull_first + r["pulls"][1]

    def thermal_of(plane):
        return ((2 * plane - count_z * NP).astype(F32)) * (1.0 / (count_z * NP))

    def row_groups():
        return [TOP + 8 * g for g in range(NR // 8)]

    def first_step(p, with_solute):
        thermal = thermal_of(k * NP + p - pull_first)
        for a in row_groups():
            rows = slice(a, a + 8)
            centre = ph[p + 2, rows, :]
            sides = [
                ph[p + 1, rows, :],
                ph[p + 3, rows, :],
                ph[p + 2, a - 1 : a + 7, :],
                ph[p + 2, a + 1 : a + 9, :],
                *lane_sides(centre),
            ]
            here = so[p + 1, rows, :]
            total = sum(sides)
            driving = driving_of(centre, total, here, thermal)
            p1[p + 1, rows, :] = advance_phase(centre, driving)
            if with_solute:
                solute_sides = [
                    so[p, rows, :],
                    so[p + 2, rows, :],
                    so[p + 1, a - 1 : a + 7, :],
                    so[p + 1, a + 1 : a + 9, :],
                    *lane_sides(here),
                ]
                mixed = sum(u * v for u, v in zip(sides, solute_sides))
                spread = sum(solute_sides) - 6.0 * here
                flux = 0.25 * ((2.0 - centre) * spread - mixed + here * total)
                rate = (DIFFUSIVITY * flux + 0.5 * (1.0 + (1.0 - PARTITION) * here) * driving) / (
                    0.5 * (1.0 + PARTITION) - 0.5 * (1.0 - PARTITION) * centre
                )
                s1[p, a - TOP : a - TOP + 8, :] = here + TIME_STEP * rate

    def second_step(p):
        plane = k * NP + p
        thermal = thermal_of(plane - pull_both)
        for a in row_groups():
            rows = slice(a, a + 8)
            centre = p1[p + 1, rows, :]
            low = jnp.where(plane == pull_both, centre, p1[p, rows, :])
            total = sum(
                [
                    low,
                    p1[p + 2, rows, :],
                    p1[p + 1, a - 1 : a + 7, :],
                    p1[p + 1, a + 1 : a + 9, :],
                    *lane_sides(centre),
                ]
            )
            driving = driving_of(centre, total, s1[p, a - TOP : a - TOP + 8, :], thermal)
            fb[p, a - TOP : a - TOP + 8, :] = advance_phase(centre, driving)

    def second_body(p, carry):
        second_step(p)
        return carry

    for p in range(NP):
        so[p + 1, TOP - 1 : TOP, :] = r["xrl"][2, p : p + 1, :]
        so[p + 1, TOP + NR : TOP + NR + 1, :] = r["xrh"][2, p : p + 1, :]

    def first_body(p, carry):
        first_step(p, True)
        return carry

    plane_row = lax.broadcasted_iota(jnp.int32, (NP, NL), 0)
    thermal_rows = (2 * (plane_row + (k * NP - pull_first)) - count_z * NP).astype(F32) * (
        1.0 / (count_z * NP)
    )

    def rows_beside(planes, with_ends):
        for side, (got, sent, at) in enumerate(
            ((r["xrl"], r["xsl"], TOP - 1), (r["xrh"], r["xsh"], TOP + NR))
        ):
            centre = got[0]
            low, high = pltpu.roll(centre, 1, 0), pltpu.roll(centre, NP - 1, 0)
            if with_ends:
                low = jnp.where(plane_row == 0, r["cru"][side : side + 1, :], low)
                high = jnp.where(plane_row == NP - 1, r["cre"][side : side + 1, :], high)
            total = sum([low, high, got[1], sent[0], *lane_sides(centre)])
            driving = driving_of(centre, total, got[2], thermal_rows)
            moved = advance_phase(centre, driving)
            for p in planes:
                p1[p + 1, at : at + 1, :] = moved[p : p + 1, :]

    lax.fori_loop(1, NP - 1, first_body, 0)
    rows_beside(range(1, NP - 1), False)
    lax.fori_loop(2, NP - 2, second_body, 0)

    @pl.when(at_top)
    def _():
        ph[NP + 2 : NP + 4] = jnp.full((2, 2 * TOP + NR, NL), FAR, F32)
        so[NP + 1 : NP + 3] = jnp.full((2, 2 * TOP + NR, NL), FAR, F32)
        r["cre"][...] = jnp.full((2, NL), FAR, F32)
        p1[NP + 2 : NP + 4] = jnp.full((2, 2 * TOP + NR, NL), FAR, F32)
        s1[NP + 1 : NP + 2] = jnp.full((1, NR, NL), FAR, F32)

    @pl.when(k == 0)
    def _():
        ph[0:2] = jnp.full((2, 2 * TOP + NR, NL), FAR, F32)
        so[0:1] = jnp.full((1, 2 * TOP + NR, NL), FAR, F32)
        r["cru"][...] = jnp.full((2, NL), FAR, F32)

    @pl.when(not_low)
    def _():
        corner_up.wait_recv()

    @pl.when(not_top)
    def _():
        corner_down.wait_recv()

    down.arrive()
    upward.arrive()

    @pl.when(not_top)
    def _():
        ph[NP + 2, own, :] = r["hrd"][0]
        ph[NP + 3, own, :] = r["hrd"][1]
        so[NP + 1, own, :] = r["hrd"][2]

    @pl.when(not_low)
    def _():
        ph[0, own, :] = r["hru"][0]
        ph[1, own, :] = r["hru"][1]
        so[0, own, :] = r["hru"][2]

    ph[1, TOP - 1 : TOP, :] = r["cru"][0:1, :]
    ph[1, TOP + NR : TOP + NR + 1, :] = r["cru"][1:2, :]
    ph[NP + 2, TOP - 1 : TOP, :] = r["cre"][0:1, :]
    ph[NP + 2, TOP + NR : TOP + NR + 1, :] = r["cre"][1:2, :]

    first_step(-1, False)
    first_step(0, True)
    first_step(NP - 1, True)
    rows_beside((0, NP - 1), True)

    @pl.when(not_top)
    def _():
        first_step(NP, False)

    @pl.when(at_top)
    def _():
        first_step(NP, True)
        for got, at in ((r["xrl"], TOP - 1), (r["xrh"], TOP + NR)):
            centre = jnp.full((NP, NL), FAR, F32)
            low = jnp.where(plane_row == 0, pltpu.roll(got[0], 1, 0), FAR)
            total = low + 5.0 * FAR
            driving = driving_of(centre, total, centre, 0.0)
            p1[NP + 1, at : at + 1, :] = advance_phase(centre, driving)[0:1, :]

    lax.fori_loop(0, 2, second_body, 0)

    def mask_of(which, local):
        return jnp.broadcast_to(which[0:1, 0:1] == local, (NR, NL))

    @pl.when(k == 0)
    def _():
        r["ixa"][...] = jnp.zeros(PIECE, jnp.int32)

    @pl.when(k > 1)
    def _():
        index_second.wait_recv()

    @pl.when(k <= 1)
    def _():
        r["ixb"][...] = jnp.zeros(PIECE, jnp.int32)

    two = r["ixb"][...] + (pull_both - k * NP)
    one = r["ixa"][...] + (pull_both - k * NP)
    none = r["ixs"][...] + (pull_both - k * NP)
    r["c2s"][0] = jnp.where(mask_of(two, 1), fb[1], fb[0])
    second.start()
    second.relay()
    lax.fori_loop(NP - 2, NP, second_body, 0)

    @pl.when(at_top)
    def _():
        second_step(NP)
        second_step(NP + 1)
        fb[NP + 2 : NP + 10] = jnp.full((8, NR, NL), FAR, F32)
        r["c2r"][0] = jnp.where(mask_of(one, NP), fb[NP], fb[NP + 1])
        r["c1r"][0] = jnp.where(
            mask_of(none, NP), fb[NP], jnp.where(mask_of(none, NP + 1), fb[NP + 1], FAR)
        )

    picked = fb[0]
    for p in range(1, NP):
        picked = jnp.where(mask_of(one, p), fb[p], picked)
    r["c1s"][0] = picked
    first.relay((1,))
    for message in bulk:
        message.relay((1,))
    second.arrive()
    beyond = jnp.broadcast_to(one[0:1, 0:1] >= NP, (NR, NL))
    r["c1s"][0] = jnp.where(beyond, r["c2r"][0], r["c1s"][0])
    first.start()
    for message in bulk:
        message.start()
    first.relay((2, 3))
    first.arrive()
    inside = jnp.broadcast_to(none[0:1, 0:1] < NP, (NR, NL))
    section = jnp.where(
        inside, jnp.where(mask_of(none, NP - 1), fb[NP - 1], fb[NP - 2]), r["c1r"][0]
    )

    for load in loads:
        load.wait()

    def exchange(src, dst, n, start):
        def one_copy(j, carry):
            other = lax.rem(i + j, count_x)
            remote(src.at[other], dst.at[i], n, {"gx": other}).start()
            return carry

        if start:
            lax.fori_loop(1, count_x, one_copy, 0)
            dst[i] = src[i]
        else:
            some = slice(0, count_x - 1)
            remote(src.at[some], dst.at[some], n, before).wait_recv()

    row_sum = jnp.sum(section, axis=1, keepdims=True)
    level = section - row_sum * (1.0 / NL)
    near, far = level[:, :HALF], level[:, HALF:]
    spectrum = jnp.concatenate([mm(near + far, r["v1"], 0), mm(near - far, r["v1"], 1)], 1)
    lane = lax.broadcasted_iota(jnp.int32, (NR, NL), 1)
    spectrum = jnp.where(lane == 0, row_sum, spectrum)
    if with_corr:
        pack(spectrum, r["sd1"])
        exchange(r["sd1"], r["rv1"], 6, True)
    for message in bulk:
        message.relay((2, 3))
    if with_corr:
        exchange(r["sd1"], r["rv1"], 6, False)

        rows = unpack(r["rv1"])
        row = lax.broadcasted_iota(jnp.int32, (NR, NL), 0)
        lowest = jnp.logical_and(row == 0, jnp.broadcast_to(i, (NR, NL)) == 0)
        mean = jnp.sum(rows, axis=1, keepdims=True) * (1.0 / NL)
        rows = jnp.where(lowest, rows - mean, rows)
        starts = [256 * g for g in range(4)]
        near = jnp.concatenate([rows[:, s : s + 128] for s in starts], 1)
        far = jnp.concatenate([rows[:, s + 128 : s + 256] for s in starts], 1)
        special_row = jnp.logical_and(
            lax.broadcasted_iota(jnp.int32, (16, HALF), 0) == 0,
            jnp.broadcast_to(i, (16, HALF)) == 0,
        )
        first_lane = lax.broadcasted_iota(jnp.int32, (16, HALF), 1) == 0
        halves = []
        for odd, part in enumerate((near + far, near - far)):
            z = mm(part, r["vcs"], odd)
            ac, as_ = z[:16, :HALF], z[:16, HALF:]
            bc, bs = z[16:, :HALF], z[16:, HALF:]
            real, imag = ac + bs, bc - as_
            power = real * real + imag * imag
            lone = ac * ac + as_ * as_
            if not odd:
                lone = jnp.where(first_lane, 0.0, lone)
            power = jnp.where(special_row, lone, power)
            halves.append(mm(jnp.concatenate([power, bc * bc + bs * bs], 0), r["vback"], odd))
        even, odd_part = halves
        lags = jnp.concatenate(
            [
                even[:, :HALF] + odd_part[:, :HALF],
                even[:, :HALF] - odd_part[:, :HALF],
            ],
            1,
        )
        sines = jnp.concatenate(
            [
                even[:16, HALF:] + odd_part[:16, HALF:],
                even[:16, HALF:] - odd_part[:16, HALF:],
            ],
            1,
        )
        special_wide = jnp.logical_and(
            lax.broadcasted_iota(jnp.int32, (16, NL), 0) == 0,
            jnp.broadcast_to(i, (16, NL)) == 0,
        )
        sines = jnp.where(special_wide, lags[16:], sines)
        pack(jnp.concatenate([lags[:16], sines], 0), r["sd2"])
        exchange(r["sd2"], r["rv2"], 7, True)
    bulk[0].arrive()
    onward.start()
    if with_corr:
        exchange(r["sd2"], r["rv2"], 7, False)
        rows = unpack(r["rv2"])
        even = jnp.concatenate([rows[:, s : s + 128] for s in starts], 1)
        odd_part = jnp.concatenate([rows[:, s + 128 : s + 256] for s in starts], 1)
        even = mm(even, r["v2"], 0)
        odd_part = mm(odd_part, r["v2"], 1)
        r["corr"][0, :, :HALF] = even + odd_part
        r["corr"][0, :, HALF:] = even - odd_part
    else:
        r["corr"][0] = section
    onward.relay()
    bulk[1].arrive()
    bulk[2].arrive()
    onward.arrive()
    r["final"][...] = fb[pl.ds(pull_both, NP)]

    for message in (down, upward, second, first, *bulk, onward):
        message.finish()
    to_before.wait_send()
    to_after.wait_send()

    @pl.when(not_top)
    def _():
        index_first.wait_send()
        corner_up.wait_send()

    @pl.when(jnp.logical_and(not_top, not_low))
    def _():
        index_second.wait_send()

    @pl.when(not_low)
    def _():
        corner_down.wait_send()

    if with_corr:
        for n, src in ((6, r["sd1"]), (7, r["sd2"])):
            some = src.at[0 : count_x - 1]
            remote(some, some, n, before).wait_send()


def per_device(run, with_corr, phase_field, solute, pull_counts, planes):
    w1, cs, back, w2 = (jnp.asarray(t) for t in tables())
    wide = 2 * TOP + NR
    vmem = lambda *shape: pltpu.VMEM(shape, F32)
    scratch = [
        vmem(NP + 4, wide, NL),
        vmem(NP + 3, wide, NL),
        vmem(NP + 4, wide, NL),
        vmem(NP + 2, NR, NL),
        vmem(18, NR, NL),
        *[vmem(3, NR, NL) for _ in range(4)],
        *[vmem(3, NP, NL) for _ in range(4)],
        *[vmem(2, NL) for _ in range(4)],
        *[pltpu.VMEM(PIECE, jnp.int32) for _ in range(3)],
        *[vmem(1, NR, NL) for _ in range(4)],
        *[vmem(32, *PIECE) for _ in range(4)],
        *[pltpu.VMEM(t.shape, BF16) for t in (w1, cs, back, w2)],
        *[vmem(n, 8, NL) for n in MESSAGES],
        pltpu.SemaphoreType.DMA((8, 4)),
        pltpu.SemaphoreType.DMA((16,)),
        pltpu.SemaphoreType.DMA((10,)),
    ]
    smem = pl.BlockSpec(memory_space=pltpu.SMEM)
    anywhere = pl.BlockSpec(memory_space=pl.ANY)
    local = pl.BlockSpec(memory_space=pltpu.VMEM)
    return pl.pallas_call(
        functools.partial(kernel, run, with_corr),
        out_shape=(
            jax.ShapeDtypeStruct((NP, NR, NL), F32),
            jax.ShapeDtypeStruct((1, NR, NL), F32),
        ),
        in_specs=[smem, smem, *[anywhere] * 6],
        out_specs=(local, local),
        scratch_shapes=scratch,
        compiler_params=pltpu.CompilerParams(
            collective_id=0, has_side_effects=True, vmem_limit_bytes=56 * 1024 * 1024
        ),
    )(pull_counts, planes, phase_field, solute, w1, cs, back, w2)


def build(mesh, run, with_corr):
    return jax.shard_map(
        functools.partial(per_device, run, with_corr),
        mesh=mesh,
        in_specs=(P("gz", "gx", None), P("gz", "gx", None), P(), P("gz")),
        out_specs=(P("gz", "gx", None), P("gz", "gx", None)),
        check_vma=False,
    )


def solution(mesh):
    return build(mesh, RUN, True)
```

time: 420 us -> 103 us (0.25)
  the two profiles are of different devices: /device:TPU:569 before, /device:TPU:57 now
where the time goes in v1:
time: 103 us
  Pallas kernels  97.6 us (95%)
  local copies, waits for them, and re-layouts  3.87 us (4%)
  between operations  1.29 us (1%)
    pallas_call x1, Pallas kernels, per_device(): pl.pallas_call(functools.partial(kernel, run, with_corr), out_shape=(jax....  97.6 us
    unnamed x2, local copies, waits for them, and re-layouts  3.87 us

profile of v1, /device:TPU:57, one launch (start us, length us, event | category | flops | bytes accessed | tf_op | source)
XLA Modules:
  0.0 102.7 jit_solution(2158500378287733181)
XLA Ops:
  1.3 97.6 %shard_map.95 = (f32[8,32,1024]{2,1,0:T(8,128)}, f32[1,32,1024]{2,1,0:T(8,128)}) custom-call(s32[2]{0:T(128)} %refs_0_.1, s32[1]{0:T(128)S(6)} %copy.12.refs_1_, f32[8,32,1024]{2,1,0:T(8,128)} %refs_2_.1, f32[8,32,1024]{2,1,0:T(8,128)} %refs_3_.1, bf16[2,2,512,512]{3,2,1,0:T(8,128)(2,1)} %constant.8.clone.refs_4_, ...), custom_call_target="tpu_custom_call" | custom-call | tf_op jit(solution)/shard_map/pallas_call | solution.py:732
  98.9 2.3 %copy.13 = f32[8,32,1024]{2,1,0:T(8,128)} copy(f32[8,32,1024]{2,1,0:T(8,128)} %get-tuple-element.4) | data formatting | bytes 2097152
  101.2 1.6 %copy.14 = f32[1,32,1024]{2,1,0:T(8,128)} copy(f32[1,32,1024]{2,1,0:T(8,128)} %get-tuple-element.5) | data formatting | bytes 262144

commit v2 on v1

--- a/solution.py
+++ b/solution.py
@@ -80,9 +80,9 @@
     return first[:rows] + first[rows:] + second
 
 
-def pack(block, out):
+def pack(block, out, base=0):
     lane_group = lax.broadcasted_iota(jnp.int32, PIECE, 1) // 32
-    for c in range(8):
+    for c in range(block.shape[1] // 128):
         v = [block[8 * g : 8 * g + 8, 128 * c : 128 * c + 128] for g in range(4)]
         for b in range(4):
             tile = v[b]
@@ -90,9 +90,7 @@
                 if g != b:
                     moved = pltpu.roll(v[g], (32 * (g - b)) % 128, 1)
                     tile = jnp.where(lane_group == g, moved, tile)
-            if b:
-                pass
-            out[4 * c + b] = tile
+            out[base + 4 * c + b] = tile
 
 
 def unpack(tiles):
@@ -101,19 +99,29 @@
     return jnp.concatenate([turned[32 * g : 32 * g + 32] for g in range(4)], 1)
 
 
-def seam_columns(run):
-    return (0, run - 1, run // 2 - 1, run // 2)
+def seam_columns(run, kind):
+    if run < 8 or kind == "small":
+        return (0, run - 1, run // 2 - 1, run // 2)
+    if kind == "onward":
+        return (0, 2, 3, 4)
+    return (0, 7, 3, 4, 2, 5, 1, 6)
+
+
+def greeting_columns(run, up):
+    kinds = ("small",) if up else ("small", "onward", "bulk")
+    return tuple(sorted({c for kind in kinds for c in seam_columns(run, kind)}))
 
 
 class Message:
-    def __init__(self, env, index, up, src, dst):
+    def __init__(self, env, index, up, src, dst, kind):
         self.src, self.dst, self.up = src, dst, up
         self.sems = [env["msem"].at[index, j] for j in range(4)]
         self.relay_ref = env["ra"][index]
         self.run, self.height = env["run"], env["height"]
         self.y = (self.run - 1 - env["y"]) if up else env["y"]
         self.h = (self.height - 1 - env["h"]) if up else env["h"]
-        self.columns = seam_columns(self.run)
+        self.columns = seam_columns(self.run, kind)
+        self.width = NL * 4 // len(self.columns)
 
     def copy(self, src, dst, send, recv, y, h):
         if self.up:
@@ -127,8 +135,15 @@
             device_id_type=MESH,
         )
 
-    def rows(self, ref, g):
-        return ref.at[:, 8 * g : 8 * g + 8, :]
+    def piece(self, ref, n):
+        g, part = n % 4, n // 4
+        return ref.at[:, 8 * g : 8 * g + 8, self.width * part : self.width * (part + 1)]
+
+    def relayed(self, early=None):
+        pieces = range(1, len(self.columns))
+        if early is None:
+            return list(pieces)
+        return [n for n in pieces if (self.columns[n] == self.run - 1) == early]
 
     def has_target(self):
         return jnp.logical_or(self.y > 0, self.h > 0)
@@ -137,7 +152,8 @@
         return jnp.logical_or(self.y < self.run - 1, self.h < self.height - 1)
 
     def start(self):
-        self.start_seam()
+        self.start_seam(True)
+        self.start_seam(False)
         self.start_inside()
 
     def start_inside(self):
@@ -145,23 +161,25 @@
         def _():
             self.copy(self.src, self.dst, 0, 1, self.y - 1, self.h).start()
 
-    def start_seam(self):
+    def start_seam(self, early):
         @pl.when(jnp.logical_and(self.y == 0, self.h > 0))
         def _():
-            for g in (2, 3, 1):
-                column = self.columns[g]
-                self.copy(self.rows(self.src, g), self.relay_ref, 0, 3, column, self.h).start()
-            end = self.run - 1
-            self.copy(self.rows(self.src, 0), self.rows(self.dst, 0), 0, 1, end, self.h - 1).start()
-
-    def relay(self, groups=(1, 2, 3)):
+            for n in self.relayed(early):
+                column = self.columns[n]
+                self.copy(self.piece(self.src, n), self.relay_ref, 0, 3, column, self.h).start()
+            if not early:
+                there = self.piece(self.dst, 0)
+                end = self.run - 1
+                self.copy(self.piece(self.src, 0), there, 0, 1, end, self.h - 1).start()
+
+    def relay(self, early=None):
         end = self.run - 1
-        for g in groups:
-
-            @pl.when(jnp.logical_and(self.h > 0, self.y == self.columns[g]))
-            def _(g=g):
+        for n in self.relayed(early):
+
+            @pl.when(jnp.logical_and(self.h > 0, self.y == self.columns[n]))
+            def _(n=n):
                 self.copy(self.relay_ref, self.relay_ref, 2, 3, end, self.h - 1).wait_recv()
-                there = self.rows(self.dst, g)
+                there = self.piece(self.dst, n)
                 self.copy(self.relay_ref, there, 2, 1, end, self.h - 1).start()
 
     def arrive(self):
@@ -174,7 +192,7 @@
         def _():
             self.copy(self.src, self.dst, 0, 1, 0, 0).wait_send()
 
-        column = [self.y == self.columns[g] for g in (1, 2, 3)]
+        column = [self.y == self.columns[n] for n in self.relayed()]
 
         @pl.when(jnp.logical_and(self.h > 0, functools.reduce(jnp.logical_or, column)))
         def _():
@@ -236,21 +254,8 @@
 
     barrier = pltpu.get_barrier_semaphore()
 
-    def greet_x(j, carry):
-        other = lax.rem(i + j, count_x)
-        pl.semaphore_signal(barrier, inc=1, device_id={"gx": other}, device_id_type=MESH)
-        return carry
-
-    lax.fori_loop(1, count_x, greet_x, 0)
-
-    def greet_y(j, carry):
-        other = h * run + lax.rem(y + j, run)
-        pl.semaphore_signal(barrier, inc=1, device_id={"gz": other}, device_id_type=MESH)
-        return carry
-
-    lax.fori_loop(1, run, greet_y, 0)
     def is_column(up):
-        return functools.reduce(jnp.logical_or, [y == (run - 1 - c if up else c) for c in seam_columns(run)])
+        return functools.reduce(jnp.logical_or, [y == (run - 1 - c if up else c) for c in greeting_columns(run, up)])
 
     def greet(other):
         pl.semaphore_signal(barrier, inc=1, device_id={"gz": other}, device_id_type=MESH)
@@ -267,11 +272,24 @@
 
         @pl.when(jnp.logical_and(far, y == last))
         def _(up=up, step=step):
-            for c in seam_columns(run):
+            for c in greeting_columns(run, up):
                 greet((h - step) * run + (run - 1 - c if up else c))
 
         greetings = greetings + jnp.where(jnp.logical_and(near, is_column(up)), 1, 0)
-        greetings = greetings + jnp.where(jnp.logical_and(far, y == last), 4, 0)
+        greetings = greetings + jnp.where(jnp.logical_and(far, y == last), len(greeting_columns(run, up)), 0)
+
+    def greet_y(j, carry):
+        other = h * run + lax.rem(y + j, run)
+        pl.semaphore_signal(barrier, inc=1, device_id={"gz": other}, device_id_type=MESH)
+        return carry
+
+    lax.fori_loop(1, run, greet_y, 0)
+    def greet_x(j, carry):
+        other = lax.rem(i + j, count_x)
+        pl.semaphore_signal(barrier, inc=1, device_id={"gx": other}, device_id_type=MESH)
+        return carry
+
+    lax.fori_loop(1, count_x, greet_x, 0)
 
     load_phase.wait()
     load_solute.wait()
@@ -297,16 +315,16 @@
         "y": y,
         "h": h,
     }
-    down = Message(env, 0, False, r["hsd"], r["hrd"])
-    upward = Message(env, 1, True, r["hsu"], r["hru"])
-    second = Message(env, 2, False, r["c2s"], r["c2r"])
-    first = Message(env, 3, False, r["c1s"], r["c1r"])
+    down = Message(env, 0, False, r["hsd"], r["hrd"], "small")
+    upward = Message(env, 1, True, r["hsu"], r["hru"], "small")
+    second = Message(env, 2, False, r["c2s"], r["c2r"], "small")
+    first = Message(env, 3, False, r["c1s"], r["c1r"], "small")
     bulk = [
-        Message(env, 4, False, fb.at[0:2], fb.at[8:10]),
-        Message(env, 5, False, fb.at[2:6], fb.at[10:14]),
-        Message(env, 6, False, fb.at[6:8], fb.at[14:16]),
+        Message(env, 4, False, fb.at[0:2], fb.at[8:10], "bulk"),
+        Message(env, 5, False, fb.at[2:6], fb.at[10:14], "bulk"),
+        Message(env, 6, False, fb.at[6:8], fb.at[14:16], "bulk"),
     ]
-    onward = Message(env, 7, False, fb.at[8:10], fb.at[16:18])
+    onward = Message(env, 7, False, fb.at[8:10], fb.at[16:18], "onward")
 
     def remote(src, dst, n, target):
         return pltpu.make_async_remote_copy(
@@ -323,8 +341,9 @@
     not_top = jnp.logical_not(at_top)
     not_low = k > 0
 
-    down.start_seam()
-    upward.start_seam()
+    for message in (down, upward):
+        message.start_seam(False)
+        message.start_seam(True)
     before = {"gx": lax.rem(i + count_x - 1, count_x)}
     after = {"gx": lax.rem(i + 1, count_x)}
     to_before = remote(r["xsl"], r["xrh"], 0, before)
@@ -568,16 +587,19 @@
     for p in range(1, NP):
         picked = jnp.where(mask_of(one, p), fb[p], picked)
     r["c1s"][0] = picked
-    first.relay((1,))
+    first.relay(True)
     for message in bulk:
-        message.relay((1,))
+        message.relay(True)
     second.arrive()
     beyond = jnp.broadcast_to(one[0:1, 0:1] >= NP, (NR, NL))
     r["c1s"][0] = jnp.where(beyond, r["c2r"][0], r["c1s"][0])
     first.start()
     for message in bulk:
-        message.start()
-    first.relay((2, 3))
+        message.start_seam(True)
+    for message in bulk:
+        message.start_seam(False)
+        message.start_inside()
+    first.relay(False)
     first.arrive()
     inside = jnp.broadcast_to(none[0:1, 0:1] < NP, (NR, NL))
     section = jnp.where(
@@ -587,32 +609,51 @@
     for load in loads:
         load.wait()
 
-    def exchange(src, dst, n, start):
+    def send_tiles(src, dst, n, first, count):
         def one_copy(j, carry):
-            other = lax.rem(i + j, count_x)
-            remote(src.at[other], dst.at[i], n, {"gx": other}).start()
+            other = first + lax.rem(i + j, count)
+
+            @pl.when(other != i)
+            def _():
+                remote(src.at[other], dst.at[i], n, {"gx": other}).start()
+
             return carry
 
-        if start:
-            lax.fori_loop(1, count_x, one_copy, 0)
-            dst[i] = src[i]
-        else:
-            some = slice(0, count_x - 1)
-            remote(src.at[some], dst.at[some], n, before).wait_recv()
+        lax.fori_loop(1, count + 1, one_copy, 0)
+
+    def await_tiles(src, dst, n):
+        dst[i] = src[i]
+        some = slice(0, count_x - 1)
+        remote(src.at[some], dst.at[some], n, before).wait_recv()
 
     row_sum = jnp.sum(section, axis=1, keepdims=True)
     level = section - row_sum * (1.0 / NL)
     near, far = level[:, :HALF], level[:, HALF:]
-    spectrum = jnp.concatenate([mm(near + far, r["v1"], 0), mm(near - far, r["v1"], 1)], 1)
-    lane = lax.broadcasted_iota(jnp.int32, (NR, NL), 1)
-    spectrum = jnp.where(lane == 0, row_sum, spectrum)
+    half = max(count_x // 2, 1)
+    even = mm(near + far, r["v1"], 0)
+    lane = lax.broadcasted_iota(jnp.int32, (NR, HALF), 1)
+    pack(jnp.where(lane == 0, row_sum, even), r["sd1"])
     if with_corr:
-        pack(spectrum, r["sd1"])
-        exchange(r["sd1"], r["rv1"], 6, True)
+        send_tiles(r["sd1"], r["rv1"], 6, 0, half)
+    pack(mm(near - far, r["v1"], 1), r["sd1"], half)
+    if with_corr:
+        send_tiles(r["sd1"], r["rv1"], 6, half, half)
     for message in bulk:
-        message.relay((2, 3))
+        message.relay(False)
+
+    @pl.when(y < run - 1)
+    def _():
+        bulk[0].arrive()
+
+    onward.start_seam(True)
+    onward.start_seam(False)
+
+    @pl.when(y < run - 1)
+    def _():
+        onward.start_inside()
+
     if with_corr:
-        exchange(r["sd1"], r["rv1"], 6, False)
+        await_tiles(r["sd1"], r["rv1"], 6)
 
         rows = unpack(r["rv1"])
         row = lax.broadcasted_iota(jnp.int32, (NR, NL), 0)
@@ -660,11 +701,16 @@
         )
         sines = jnp.where(special_wide, lags[16:], sines)
         pack(jnp.concatenate([lags[:16], sines], 0), r["sd2"])
-        exchange(r["sd2"], r["rv2"], 7, True)
-    bulk[0].arrive()
-    onward.start()
+        send_tiles(r["sd2"], r["rv2"], 7, 0, count_x)
+    onward.relay()
+
+    @pl.when(y == run - 1)
+    def _():
+        bulk[0].arrive()
+        onward.start_inside()
+
     if with_corr:
-        exchange(r["sd2"], r["rv2"], 7, False)
+        await_tiles(r["sd2"], r["rv2"], 7)
         rows = unpack(r["rv2"])
         even = jnp.concatenate([rows[:, s : s + 128] for s in starts], 1)
         odd_part = jnp.concatenate([rows[:, s + 128 : s + 256] for s in starts], 1)
@@ -674,7 +720,6 @@
         r["corr"][0, :, HALF:] = even - odd_part
     else:
         r["corr"][0] = section
-    onward.relay()
     bulk[1].arrive()
     bulk[2].arrive()
     onward.arrive()
@@ -702,6 +747,11 @@
         for n, src in ((6, r["sd1"]), (7, r["sd2"])):
             some = src.at[0 : count_x - 1]
             remote(some, some, n, before).wait_send()
+
+
+def hand_over(final_in, corr_in, final_out, corr_out):
+    final_out[...] = final_in[...]
+    corr_out[...] = corr_in[...]
 
 
 def per_device(run, with_corr, phase_field, solute, pull_counts, planes):
@@ -721,7 +771,10 @@
         *[vmem(1, NR, NL) for _ in range(4)],
         *[vmem(32, *PIECE) for _ in range(4)],
         *[pltpu.VMEM(t.shape, BF16) for t in (w1, cs, back, w2)],
-        *[vmem(n, 8, NL) for n in MESSAGES],
+        *[
+            vmem(n, 8, NL * 4 // len(seam_columns(run, kind)))
+            for n, kind in zip(MESSAGES, ["small"] * 4 + ["bulk"] * 3 + ["onward"])
+        ],
         pltpu.SemaphoreType.DMA((8, 4)),
         pltpu.SemaphoreType.DMA((16,)),
         pltpu.SemaphoreType.DMA((10,)),
@@ -729,7 +782,7 @@
     smem = pl.BlockSpec(memory_space=pltpu.SMEM)
     anywhere = pl.BlockSpec(memory_space=pl.ANY)
     local = pl.BlockSpec(memory_space=pltpu.VMEM)
-    return pl.pallas_call(
+    final, corr = pl.pallas_call(
         functools.partial(kernel, run, with_corr),
         out_shape=(
             jax.ShapeDtypeStruct((NP, NR, NL), F32),
@@ -742,6 +795,15 @@
             collective_id=0, has_side_effects=True, vmem_limit_bytes=56 * 1024 * 1024
         ),
     )(pull_counts, planes, phase_field, solute, w1, cs, back, w2)
+    return pl.pallas_call(
+        hand_over,
+        out_shape=(
+            jax.ShapeDtypeStruct((NP, NR, NL), F32),
+            jax.ShapeDtypeStruct((1, NR, NL), F32),
+        ),
+        in_specs=[local, local],
+        out_specs=(local, local),
+    )(final, corr)
 
 
 def build(mesh, run, with_corr):

time: 103 us -> 89.8 us (0.87)
  the two profiles are of different devices: /device:TPU:57 before, /device:TPU:320 now
where the time goes in v2:
time: 89.8 us; the launch traced here: 89.6 us
  Pallas kernels  88.3 us (98%)
  between operations  1.29 us (1%)
    pallas_call x1, Pallas kernels, per_device(): pl.pallas_call(functools.partial(kernel, run, with_corr), out_shape=(jax....  86 us
    pallas_call x1, Pallas kernels, per_device(): pl.pallas_call(hand_over, out_shape=(jax.ShapeDtypeStruct((NP, NR, NL), F...  2.3 us

profile of v2, /device:TPU:320, one launch (start us, length us, event | category | flops | bytes accessed | tf_op | source)
XLA Modules:
  0.0 89.6 jit_solution(2723243816990218348)
XLA Ops:
  1.3 86.0 %shard_map.95 = (f32[8,32,1024]{2,1,0:T(8,128)}, f32[1,32,1024]{2,1,0:T(8,128)}) custom-call(s32[2]{0:T(128)} %refs_0_.1, s32[1]{0:T(128)S(6)} %copy.10.refs_1_, f32[8,32,1024]{2,1,0:T(8,128)} %refs_2_.1, f32[8,32,1024]{2,1,0:T(8,128)} %refs_3_.1, bf16[2,2,512,512]{3,2,1,0:T(8,128)(2,1)} %constant.8.clone.refs_4_, ...), custom_call_target="tpu_custom_call" | custom-call | tf_op jit(solution)/shard_map/pallas_call | solution.py:785
  87.3 2.3 %shard_map.96 = (f32[8,32,1024]{2,1,0:T(8,128)}, f32[1,32,1024]{2,1,0:T(8,128)}) custom-call(f32[8,32,1024]{2,1,0:T(8,128)} %get-tuple-element.4.final_in, f32[1,32,1024]{2,1,0:T(8,128)} %get-tuple-element.5.corr_in), custom_call_target="tpu_custom_call" | custom-call | tf_op jit(solution)/shard_map/pallas_call | solution.py:798

commit v3 on v2

--- a/solution.py
+++ b/solution.py
@@ -104,7 +104,7 @@
         return (0, run - 1, run // 2 - 1, run // 2)
     if kind == "onward":
         return (0, 2, 3, 4)
-    return (0, 7, 3, 4, 2, 5, 1, 6)
+    return (0, 7, 3, 4, 0, 5, 1, 6)
 
 
 def greeting_columns(run, up):
@@ -140,9 +140,9 @@
         return ref.at[:, 8 * g : 8 * g + 8, self.width * part : self.width * (part + 1)]
 
     def relayed(self, early=None):
-        pieces = range(1, len(self.columns))
+        pieces = [n for n, c in enumerate(self.columns) if c > 0]
         if early is None:
-            return list(pieces)
+            return pieces
         return [n for n in pieces if (self.columns[n] == self.run - 1) == early]
 
     def has_target(self):
@@ -167,10 +167,11 @@
             for n in self.relayed(early):
                 column = self.columns[n]
                 self.copy(self.piece(self.src, n), self.relay_ref, 0, 3, column, self.h).start()
-            if not early:
-                there = self.piece(self.dst, 0)
+            direct = [] if early else [n for n, c in enumerate(self.columns) if c == 0]
+            for n in direct:
+                there = self.piece(self.dst, n)
                 end = self.run - 1
-                self.copy(self.piece(self.src, 0), there, 0, 1, end, self.h - 1).start()
+                self.copy(self.piece(self.src, n), there, 0, 1, end, self.h - 1).start()
 
     def relay(self, early=None):
         end = self.run - 1
@@ -588,8 +589,6 @@
         picked = jnp.where(mask_of(one, p), fb[p], picked)
     r["c1s"][0] = picked
     first.relay(True)
-    for message in bulk:
-        message.relay(True)
     second.arrive()
     beyond = jnp.broadcast_to(one[0:1, 0:1] >= NP, (NR, NL))
     r["c1s"][0] = jnp.where(beyond, r["c2r"][0], r["c1s"][0])
@@ -600,6 +599,8 @@
         message.start_seam(False)
         message.start_inside()
     first.relay(False)
+    for message in bulk:
+        message.relay(True)
     first.arrive()
     inside = jnp.broadcast_to(none[0:1, 0:1] < NP, (NR, NL))
     section = jnp.where(
@@ -641,16 +642,12 @@
     for message in bulk:
         message.relay(False)
 
-    @pl.when(y < run - 1)
+    @pl.when(y == 0)
     def _():
         bulk[0].arrive()
 
     onward.start_seam(True)
     onward.start_seam(False)
-
-    @pl.when(y < run - 1)
-    def _():
-        onward.start_inside()
 
     if with_corr:
         await_tiles(r["sd1"], r["rv1"], 6)
@@ -704,7 +701,7 @@
         send_tiles(r["sd2"], r["rv2"], 7, 0, count_x)
     onward.relay()
 
-    @pl.when(y == run - 1)
+    @pl.when(y > 0)
     def _():
         bulk[0].arrive()
         onward.start_inside()

time: 89.8 us -> 89.3 us (level)
  the two profiles are of different devices: /device:TPU:320 before, /device:TPU:1 now
where the time goes in v3:
time: 89.3 us; the launch traced here: 89.1 us
  Pallas kernels  87.9 us (98%)
  between operations  1.29 us (1%)
    pallas_call x1, Pallas kernels, per_device(): pl.pallas_call(functools.partial(kernel, run, with_corr), out_shape=(jax....  85.6 us
    pallas_call x1, Pallas kernels, per_device(): pl.pallas_call(hand_over, out_shape=(jax.ShapeDtypeStruct((NP, NR, NL), F...  2.3 us

profile of v3, /device:TPU:1, one launch (start us, length us, event | category | flops | bytes accessed | tf_op | source)
XLA Modules:
  0.0 89.1 jit_solution(12818013885322338777)
XLA Ops:
  1.3 85.6 %shard_map.95 = (f32[8,32,1024]{2,1,0:T(8,128)}, f32[1,32,1024]{2,1,0:T(8,128)}) custom-call(s32[2]{0:T(128)} %refs_0_.1, s32[1]{0:T(128)S(6)} %copy.10.refs_1_, f32[8,32,1024]{2,1,0:T(8,128)} %refs_2_.1, f32[8,32,1024]{2,1,0:T(8,128)} %refs_3_.1, bf16[2,2,512,512]{3,2,1,0:T(8,128)(2,1)} %constant.8.clone.refs_4_, ...), custom_call_target="tpu_custom_call" | custom-call | tf_op jit(solution)/shard_map/pallas_call | solution.py:782
  86.8 2.3 %shard_map.96 = (f32[8,32,1024]{2,1,0:T(8,128)}, f32[1,32,1024]{2,1,0:T(8,128)}) custom-call(f32[8,32,1024]{2,1,0:T(8,128)} %get-tuple-element.4.final_in, f32[1,32,1024]{2,1,0:T(8,128)} %get-tuple-element.5.corr_in), custom_call_target="tpu_custom_call" | custom-call | tf_op jit(solution)/shard_map/pallas_call | solution.py:795
